TPU v7x, 512 devices: a whole 4x4x16 slice. The times are simulated.
512 devices in a mesh: pipe: 2 (over core), dp: 16 (over y, x), tensor: 16 (over z).
Axes of the slice: x: 4, y: 4, z: 16, core: 2. Of those that a mesh axis runs over, the one named last changes fastest.
Arguments:
- x_act: bfloat16 [2, 6144, 16384], P('pipe', 'dp', 'tensor'), may hold values from -6 to 6
- grad_z: bfloat16 [2, 6144, 26624], P('pipe', 'dp', 'tensor'), may hold values from -6 to 6
- weight_tiles: bfloat16 [2, 256, 128, 128], P('pipe', 'tensor'), may hold values from -0.5 to 0.5
- tile_rows: int32 [2, 256], P('pipe', 'tensor'), may hold values from 0 to 127, as said below
- tile_cols: int32 [2, 256], P('pipe', 'tensor'), may hold values from 0 to 12
- err_in: float32 [2, 16, 256, 128, 128], P('pipe', 'dp', 'tensor'), may hold values from -0.3 to 0.3
- kept_mask: int32 [2, 16, 256], P('pipe', 'dp', 'tensor'), may hold values 0 or 1
- tile_list: int32 [2, 16, 192], P('pipe', 'dp', 'tensor'), may hold values from 0 to 23, as said below
- live_count: int32 [2, 16, 16], P('pipe', 'dp', 'tensor'), may hold values from 1 to 12, as said below
Outputs:
- recv_tiles: bfloat16 [2, 16, 192, 128, 128], P('pipe', 'dp', 'tensor')
- err_out: float32 [2, 16, 256, 128, 128], P('pipe', 'dp', 'tensor')
- grad_sum: float32 [2, 16, 16, 128, 128], P('pipe', 'dp', 'tensor')
Inputs may be any that keep to these rules, and one draw needn't show every extreme that they name: `tile_rows`: entry j of a tensor rank's 16 entries of one section names a column block held by tensor rank j // (16 / 16), that is one of the blocks ((j // (16 / 16)) * L to that plus L - 1, L = 16384 / (128 * 16)). `tile_list`: A device's 12 entries are distinct tile numbers m * L + b of its own region (L = 16384 / (128 * 16), m < 3, b < L). `live_count`: some device uses all 12 entries of its list.
All inputs are finite; a program needn't handle non-finite values. No bound on the sum of `kept_mask` on one device may be relied on, other than what follows from the above.
Results may differ from a plain program's by a relative error of at most 0.0048.
Values may be sent and summed in bfloat16 or wider, within the bound.
A program may use at most 128 MiB of HBM per device.

v0:
```python
import jax
import jax.numpy as jnp
from jax import lax
from jax.sharding import PartitionSpec as P


def shifted(value, axis, by):
    count = lax.axis_size(axis)
    return lax.ppermute(value, axis, [(i, (i + by) % count) for i in range(count)])


def pack_listed(input_grad, listed, live_now, tile_size, local_blocks):
    tok_count = input_grad.shape[0]
    grid = input_grad.reshape(tok_count // tile_size, tile_size, local_blocks, tile_size)
    picked = grid[listed // local_blocks, :, listed % local_blocks, :]
    valid = jnp.arange(listed.shape[0], dtype=jnp.int32) < live_now[0]
    return jnp.where(valid[:, None, None], picked, jnp.zeros_like(picked))


def local(
    x_act, grad_z, weight_tiles, tile_rows, tile_cols, err_in, kept_mask, tile_list, live_count
):
    tensor_count = lax.axis_size("tensor")
    inputs = x_act[0]
    grads_out = grad_z[0]
    stored = weight_tiles[0]
    row_ids = tile_rows[0]
    col_ids = tile_cols[0]
    tok_count = inputs.shape[0]
    tile_size = stored.shape[1]
    local_blocks = inputs.shape[1] // tile_size
    local_rows = row_ids % local_blocks
    grad_blocks = grads_out.reshape(tok_count, grads_out.shape[1] // tile_size, tile_size)
    grad_sel = jnp.take(grad_blocks, col_ids, axis=1)
    gathered = lax.all_gather(inputs, "tensor", axis=1, tiled=True)
    input_sel = jnp.take(
        gathered.reshape(tok_count, local_blocks * tensor_count, tile_size), row_ids, axis=1
    )
    weight_grads = jnp.einsum(
        "tkc,tkf->kcf", input_sel, grad_sel, preferred_element_type=jnp.float32
    ) * (1.0 / tok_count)
    accumulated = weight_grads + err_in[0, 0]
    keep_now = (kept_mask[0, 0] == 1)[:, None, None]
    sent_tiles = jnp.where(keep_now, accumulated, jnp.float32(0.0))
    residual = accumulated - sent_tiles
    summed = lax.psum_scatter(sent_tiles, "dp", scatter_dimension=0, tiled=True)
    partial_value = jnp.einsum(
        "tkf,kcf->tkc", grad_sel, stored, preferred_element_type=jnp.float32
    ).astype(jnp.bfloat16)
    arrived_terms, arrived_rows = (
        lax.all_to_all(partial_value, "tensor", split_axis=1, concat_axis=1, tiled=True),
        lax.all_to_all(local_rows[None, :], "tensor", split_axis=1, concat_axis=1, tiled=True),
    )
    onehot = (
        arrived_rows[0][:, None] == jnp.arange(local_blocks, dtype=jnp.int32)[None, :]
    ).astype(jnp.bfloat16)
    input_grad = jnp.einsum(
        "trc,rb->tbc", arrived_terms, onehot, preferred_element_type=jnp.float32
    ).astype(jnp.bfloat16)
    listed = tile_list[0, 0]
    live_now = live_count[0, 0]
    grad_in, listed_in, live_in = shifted((input_grad, listed, live_now), "pipe", -1)
    arrived = pack_listed(grad_in, listed_in, live_in, tile_size, local_blocks)
    return (arrived[None, None], residual[None, None], summed[None, None])


def solution(mesh):
    return jax.shard_map(
        local,
        mesh=mesh,
        in_specs=(
            P("pipe", "dp", "tensor"),
            P("pipe", "dp", "tensor"),
            P("pipe", "tensor", None, None),
            P("pipe", "tensor"),
            P("pipe", "tensor"),
            P("pipe", "dp", "tensor", None, None),
            P("pipe", "dp", "tensor"),
            P("pipe", "dp", "tensor"),
            P("pipe", "dp", "tensor"),
        ),
        out_specs=(
            P("pipe", "dp", "tensor", None, None),
            P("pipe", "dp", "tensor", None, None),
            P("pipe", "dp", "tensor", None, None),
        ),
        check_vma=False,
    )
```

profile of v0, /device:TPU:2, one launch (start us, length us, event | category | flops | bytes accessed | tf_op | source)
XLA Modules:
  0.0 350.0 jit_solution(13440303011730557698)
XLA Ops:
  7.2 0.0 copy-start
  7.2 0.0 copy-start.5
  7.2 0.0 copy-start.2
  7.2 0.0 all-gather.3.cloned.1.call-start
  7.2 2.4 copy.37
  9.7 0.0 all-gather.3.cloned.1.call-update
  9.7 0.0 copy-done.5
  9.7 0.7 copy.32
  10.4 15.2 %all-to-all-start = ((s32[1,16,1]{2,0,1:T(1,128)}), s32[1,16,1]{2,0,1:T(1,128)S(1)}, u32[]{:S(2)}, u32[]{:S(2)}) async-start(s32[1,16,1]{2,0,1:T(1,128)} %copy.32), calls=%async_computation | async-start | bytes 16384 | tf_op jit(solution)/shard_map/all_to_all | solution.py:52
  25.6 0.0 copy-done.2
  25.6 1.7 copy.33
  27.3 0.0 copy-start.4
  27.3 2.1 copy.34
  29.4 0.0 copy-done.4
  29.4 0.9 gather_fusion
  30.3 0.0 copy-start.1
  30.3 0.0 copy-done
  30.3 1.8 fusion.8
  32.1 0.0 copy-done.1
  32.1 0.0 copy-start.6
  32.1 5.8 %all-to-all-done = s32[1,16,1]{2,0,1:T(1,128)S(1)} async-done(((s32[1,16,1]{2,0,1:T(1,128)}), s32[1,16,1]{2,0,1:T(1,128)S(1)}, u32[]{:S(2)}, u32[]{:S(2)}) %all-to-all-start) | async-done | bytes 96 | tf_op jit(solution)/shard_map/all_to_all | solution.py:52
  38.0 6.3 %all-to-all-start.1 = ((bf16[384,16,128]{2,0,1:T(8,128)(2,1)}), bf16[384,16,128]{2,0,1:T(8,128)(2,1)S(1)}, u32[]{:S(2)}, u32[]{:S(2)}) async-start(bf16[384,16,128]{2,0,1:T(8,128)(2,1)} %fusion.8), calls=%async_computation.1 | async-start | bytes 3145728 | tf_op jit(solution)/shard_map/all_to_all | solution.py:51
  44.3 0.0 reduce-scatter.4.cloned.1.call-start
  44.4 0.0 copy-done.6
  44.4 186.3 %all-gather.3.cloned.1.call-done = bf16[1,384,16384]{1,2,0:T(8,128)(2,1)} async-done(((bf16[1,384,1024]{1,2,0:T(8,128)(2,1)}), bf16[1,384,16384]{1,2,0:T(8,128)(2,1)}) %all-gather.3.cloned.1.call-update) | async-done | bytes 12582928 | tf_op jit(solution)/shard_map/all_gather | solution.py:35
  230.7 15.8 %copy.38 = bf16[384,128,128]{2,0,1:T(8,128)(2,1)} copy(bf16[384,128,128]{0,2,1:T(8,128)(2,1)} %bitcast.64) | data formatting | bytes 25165824 | tf_op jit(solution)/shard_map/reshape | solution.py:37
  246.5 0.0 copy-start.3
  246.5 6.6 %gather_fusion.2 = bf16[16,384,128]{2,1,0:T(8,128)(2,1)} fusion(bf16[384,128,128]{2,0,1:T(8,128)(2,1)} %copy.38, s32[1024]{0:T(1024)S(1)} %pad_clamp_fusion), kind=kCustom, calls=%fused_computation.2 | custom fusion | bytes 3145792 | tf_op jit(solution)/shard_map/jit(_take)/gather | solution.py:36
  253.1 0.0 copy-done.3
  253.1 4.1 %broadcast_select_fusion.3 = (f32[16,128,128]{2,1,0:T(8,128)}, f32[1,1,16,128,128]{4,3,2,1,0:T(8,128)}) fusion(pred[16]{0:T(512)(128)(4,1)S(1)} %compare_bitcast_fusion, f32[1,1,16,128,128]{4,3,2,1,0:T(8,128)S(1)} %copy-done.3, bf16[16,384,128]{2,1,0:T(8,128)(2,1)} %copy-done.1, pred[16]{0:T(512)(128)(4,1)S(1)} %compare_and_fusion.1, ...), kind=kOutput, calls=%fused_computation.21 | convolution fusion | flops 203948032 | bytes 6291504 | tf_op jit(solution)/shard_map/tkc,tkf->kcf/dot_general | solution.py:39
  257.2 0.0 copy-start.7
  257.2 0.0 reduce-scatter.4.cloned.1.call-update
  257.2 0.4 reduce
  257.6 0.0 all-to-all-done.1
  257.6 0.9 fusion.24
  258.6 1.9 collective-permute-start.1
  260.5 0.0 copy-done.7
  260.5 2.4 collective-permute-start.2
  262.9 1.9 collective-permute-start
  264.9 1.4 collective-permute-done
  266.2 0.6 iota_compare_fusion.1
  266.9 0.0 collective-permute-done.2
  266.9 0.0 collective-permute-done.1
  266.9 0.2 copy.36
  267.1 0.7 gather_fusion.1
  267.8 0.8 bitcast_select_fusion
  268.6 74.6 %reduce-scatter.4.cloned.1.call-done = f32[1,128,128]{2,1,0:T(8,128)} async-done(((f32[16,128,128]{2,1,0:T(8,128)}), f32[1,128,128]{2,1,0:T(8,128)}) %reduce-scatter.4.cloned.1.call-update) | async-done | bytes 65552
  (9 shorter events, 0.1 us)
Async XLA Ops:
  7.2 23.1 %copy-start = (bf16[1,16,128,128]{3,2,1,0:T(8,128)(2,1)S(1)}, bf16[1,16,128,128]{3,2,1,0:T(8,128)(2,1)}, u32[]{:S(2)}) copy-start(bf16[1,16,128,128]{3,2,1,0:T(8,128)(2,1)} %param.11) | copy-start | bytes 1572868
  7.2 2.5 copy-start.5
  7.2 18.4 %copy-start.2 = (bf16[1,384,1664]{2,1,0:T(8,128)(2,1)S(1)}, bf16[1,384,1664]{2,1,0:T(8,128)(2,1)}, u32[]{:S(2)}) copy-start(bf16[1,384,1664]{2,1,0:T(8,128)(2,1)} %param.10) | copy-start | bytes 3833860
  7.2 223.5 %all-gather.3.cloned.1.call-start = ((), (), s32[]{:S(2)}) async-start(), calls=%async_computation.3 | async-start | bytes 13369344 | tf_op jit(solution)/shard_map/all_gather | solution.py:35
  10.4 27.6 %all-to-all-start = ((s32[1,16,1]{2,0,1:T(1,128)}), s32[1,16,1]{2,0,1:T(1,128)S(1)}, u32[]{:S(2)}, u32[]{:S(2)}) async-start(s32[1,16,1]{2,0,1:T(1,128)} %copy.32), calls=%async_computation | async-start | bytes 16384 | tf_op jit(solution)/shard_map/all_to_all | solution.py:52
  27.3 2.1 copy-start.4
  30.3 1.9 copy-start.1
  32.1 12.3 %copy-start.6 = (s32[1,1,16]{2,1,0:T(1,128)S(1)}, s32[1,1,16]{2,1,0:T(1,128)}, u32[]{:S(2)}) copy-start(s32[1,1,16]{2,1,0:T(1,128)} %param.15) | copy-start | bytes 196
  38.0 219.7 %all-to-all-start.1 = ((bf16[384,16,128]{2,0,1:T(8,128)(2,1)}), bf16[384,16,128]{2,0,1:T(8,128)(2,1)S(1)}, u32[]{:S(2)}, u32[]{:S(2)}) async-start(bf16[384,16,128]{2,0,1:T(8,128)(2,1)} %fusion.8), calls=%async_computation.1 | async-start | bytes 3145728 | tf_op jit(solution)/shard_map/all_to_all | solution.py:51
  44.3 298.9 %reduce-scatter.4.cloned.1.call-start = ((), (), s32[]{:S(2)}) async-start(), calls=%async_computation.4 | async-start | bytes 1114112
  246.5 6.6 %copy-start.3 = (f32[1,1,16,128,128]{4,3,2,1,0:T(8,128)S(1)}, f32[1,1,16,128,128]{4,3,2,1,0:T(8,128)}, u32[]{:S(2)}) copy-start(f32[1,1,16,128,128]{4,3,2,1,0:T(8,128)} %param.14) | copy-start | bytes 3145732
  257.2 3.3 copy-start.7
  258.6 8.3 %collective-permute-start.1 = (bf16[384,8,128]{2,1,0:T(8,128)(2,1)S(1)}, bf16[384,8,128]{2,1,0:T(8,128)(2,1)S(1)}, u32[]{:S(2)}, u32[]{:S(2)}) collective-permute-start(bf16[384,8,128]{2,1,0:T(8,128)(2,1)S(1)} %fusion.24), channel_id=1, source_target_pairs={{0,256},{256,0},{1,257},{257,1},{2,258},{258,2},{3,259},{259,3},{4... | collective-permute-start | bytes 2359304 | tf_op jit(solution)/shard_map/ppermute | solution.py:9
  260.5 6.3 %collective-permute-start.2 = (s32[12]{0:T(128)S(1)}, s32[12]{0:T(128)S(1)}, u32[]{:S(2)}, u32[]{:S(2)}) collective-permute-start(s32[12]{0:T(128)S(1)} %bitcast.68), channel_id=1, source_target_pairs={{0,256},{256,0},{1,257},{257,1},{2,258},{258,2},{3,259},{259,3},{4... | collective-permute-start | bytes 152 | tf_op jit(solution)/shard_map/ppermute | solution.py:9
  262.9 3.3 collective-permute-start
Sparse Core Ops, SparseCore 0:
  10.7 219.9 all-gather.2
  257.4 85.7 reduce-scatter.3
where the time goes:
time: 351 us; the launch traced here: 350 us
  waiting for transfers between devices  268 us (76%)
  local copies, waits for them, and re-layouts  31 us (9%)
  starting transfers between devices  27.9 us (8%)
  between operations  14.3 us (4%)
  matrix products  6.86 us (2%)
    all_gather x1, waiting for transfers between devices, local(): gathered = lax.all_gather(inputs, 'tensor', axis=1, tiled=True)  186 us
    unnamed x3, waiting for transfers between devices  74.6 us
    reshape x1, local copies, waits for them, and re-layouts, local(): gathered.reshape(tok_count, local_blocks * tensor_count, tile_size)  15.8 us
    all_to_all x1, starting transfers between devices, local(): lax.all_to_all(local_rows[None, :], 'tensor', split_axis=1, concat_axis=1...  15.2 us
  transfers between devices with their start and end apart: 7, of which 4 were waited for; matrix products, arithmetic and copies ran while one was open for 11% of the time, Pallas kernels for 0%

commit v1 on v0

--- a/solution.py
+++ b/solution.py
@@ -32,7 +32,9 @@
     local_rows = row_ids % local_blocks
     grad_blocks = grads_out.reshape(tok_count, grads_out.shape[1] // tile_size, tile_size)
     grad_sel = jnp.take(grad_blocks, col_ids, axis=1)
-    gathered = lax.all_gather(inputs, "tensor", axis=1, tiled=True)
+    gathered = jnp.concatenate(
+        lax.all_to_all(jnp.stack([inputs] * lax.axis_size("tensor")), "tensor", 0, 0), axis=1
+    )
     input_sel = jnp.take(
         gathered.reshape(tok_count, local_blocks * tensor_count, tile_size), row_ids, axis=1
     )

time: 351 us -> 722 us (2.06)
  waiting for transfers between devices: 268 us -> 624 us
  starting transfers between devices: 27.9 us -> 37.2 us
    all_to_all x0 -> x1, waiting for transfers between devices: none -> 534 us  [local(): lax.all_to_all(jnp.stack([inputs] * lax.axis_size('tensor')), 'tensor', 0...]
    all_gather x1 -> x0, waiting for transfers between devices: 186 us -> none  [local(): gathered = lax.all_gather(inputs, 'tensor', axis=1, tiled=True)]
    all_to_all x1, waiting for transfers between devices: 0.01 us -> 47.3 us  [local(): lax.all_to_all(partial_value, 'tensor', split_axis=1, concat_axis=1, tile...]
    unnamed x3 -> x2, waiting for transfers between devices: 74.6 us -> 30.9 us
    another operation x0 -> x3, local copies, waits for them, and re-layouts: none -> 23.3 us  [the longest x1 15.7 us: local(): gathered.reshape(tok_count, local_blocks * tensor_count, tile_size)]
    reshape x1 -> x0, local copies, waits for them, and re-layouts: 15.8 us -> none  [local(): gathered.reshape(tok_count, local_blocks * tensor_count, tile_size)]
  transfers between devices with their start and end apart: 7 -> 7, of which waited for: 4 -> 5; matrix products, arithmetic and copies ran while one was open for 11% -> 5% of each run, Pallas kernels for 0% -> 0%
where the time goes in v1:
time: 722 us; the launch traced here: 721 us
  waiting for transfers between devices  624 us (86%)
  starting transfers between devices  37.2 us (5%)
  local copies, waits for them, and re-layouts  36.1 us (5%)
  between operations  14.3 us (2%)
    all_to_all x1, waiting for transfers between devices, local(): lax.all_to_all(jnp.stack([inputs] * lax.axis_size('tensor')), 'tensor', 0...  534 us
    all_to_all x1, waiting for transfers between devices, local(): lax.all_to_all(partial_value, 'tensor', split_axis=1, concat_axis=1, tile...  47.3 us
    unnamed x2, waiting for transfers between devices  30.9 us
    another operation x1, local copies, waits for them, and re-layouts, local(): gathered.reshape(tok_count, local_blocks * tensor_count, tile_size)  15.7 us
    all_to_all x1, starting transfers between devices, local(): lax.all_to_all(local_rows[None, :], 'tensor', split_axis=1, concat_axis=1...  15.2 us
  transfers between devices with their start and end apart: 7, of which 5 were waited for; matrix products, arithmetic and copies ran while one was open for 5% of the time, Pallas kernels for 0%

profile of v1, /device:TPU:2, one launch (start us, length us, event | category | flops | bytes accessed | tf_op | source)
XLA Modules:
  0.0 721.4 jit_solution(13819748071034006781)
XLA Ops:
  7.2 0.0 copy-start
  7.2 0.7 fusion.32
  7.9 0.7 copy.27
  8.6 15.2 %all-to-all-start = ((s32[1,16,1]{2,0,1:T(1,128)}), s32[1,16,1]{2,0,1:T(1,128)S(1)}, u32[]{:S(2)}, u32[]{:S(2)}) async-start(s32[1,16,1]{2,0,1:T(1,128)} %copy.27), calls=%async_computation | async-start | bytes 16384 | tf_op jit(solution)/shard_map/all_to_all | solution.py:54
  23.8 1.5 copy.32
  25.3 10.9 %all-to-all-done = s32[1,16,1]{2,0,1:T(1,128)S(1)} async-done(((s32[1,16,1]{2,0,1:T(1,128)}), s32[1,16,1]{2,0,1:T(1,128)S(1)}, u32[]{:S(2)}, u32[]{:S(2)}) %all-to-all-start) | async-done | bytes 96 | tf_op jit(solution)/shard_map/all_to_all | solution.py:54
  36.1 6.1 stack.3
  42.2 0.0 copy-start.2
  42.2 5.1 all-to-all-start.2
  47.3 0.0 copy-done.2
  47.3 1.7 copy.28
  49.0 0.0 copy-start.4
  49.1 2.1 copy.29
  51.1 0.0 copy-done.4
  51.2 0.9 gather_fusion
  52.0 0.0 copy-start.1
  52.0 0.0 copy-done
  52.1 1.8 fusion.8
  53.9 0.0 copy-done.1
  53.9 0.0 copy-start.5
  53.9 0.0 copy-start.6
  53.9 534.1 %all-to-all-done.2 = bf16[16,384,1024]{1,2,0:T(8,128)(2,1)} async-done(((bf16[16,384,1024]{1,2,0:T(8,128)(2,1)}), bf16[16,384,1024]{1,2,0:T(8,128)(2,1)}, u32[]{:S(2)}, u32[]{:S(2)}) %all-to-all-start.2) | async-done | bytes 12582944 | tf_op jit(solution)/shard_map/all_to_all | solution.py:36
  588.0 10.6 %all-to-all-start.1 = ((bf16[384,16,128]{2,0,1:T(8,128)(2,1)}), bf16[384,16,128]{2,0,1:T(8,128)(2,1)S(1)}, u32[]{:S(2)}, u32[]{:S(2)}) async-start(bf16[384,16,128]{2,0,1:T(8,128)(2,1)} %fusion.8), calls=%async_computation.1 | async-start | bytes 3145728 | tf_op jit(solution)/shard_map/all_to_all | solution.py:53
  598.6 0.0 reduce-scatter.4.cloned.1.call-start
  598.6 0.0 copy-done.5
  598.7 0.0 copy-done.6
  598.7 15.7 %copy.33 = bf16[384,128,128]{2,0,1:T(8,128)(2,1)} copy(bf16[384,128,128]{0,2,1:T(8,128)(2,1)} %bitcast.18) | data formatting | bytes 25165824 | tf_op jit(solution)/shard_map/reshape;reshape | solution.py:39
  614.5 0.0 copy-start.3
  614.5 6.6 gather_fusion.2
  621.0 0.0 copy-done.3
  621.0 4.1 broadcast_select_fusion.3
  625.1 0.0 copy-start.7
  625.1 0.0 reduce-scatter.4.cloned.1.call-update
  625.1 0.4 reduce
  625.5 47.3 %all-to-all-done.1 = bf16[384,16,128]{2,0,1:T(8,128)(2,1)S(1)} async-done(((bf16[384,16,128]{2,0,1:T(8,128)(2,1)}), bf16[384,16,128]{2,0,1:T(8,128)(2,1)S(1)}, u32[]{:S(2)}, u32[]{:S(2)}) %all-to-all-start.1) | async-done | bytes 1572896 | tf_op jit(solution)/shard_map/all_to_all | solution.py:53
  672.9 0.9 fusion.24
  673.8 1.9 collective-permute-start.1
  675.7 0.0 copy-done.7
  675.8 2.4 collective-permute-start.2
  678.2 1.9 collective-permute-start
  680.1 1.2 collective-permute-done
  681.3 0.6 iota_compare_fusion.1
  681.9 0.0 collective-permute-done.2
  682.0 0.0 collective-permute-done.1
  682.0 0.2 copy.31
  682.1 0.7 gather_fusion.1
  682.8 0.8 bitcast_select_fusion
  683.7 30.9 %reduce-scatter.4.cloned.1.call-done = f32[1,128,128]{2,1,0:T(8,128)} async-done(((f32[16,128,128]{2,1,0:T(8,128)}), f32[1,128,128]{2,1,0:T(8,128)}) %reduce-scatter.4.cloned.1.call-update) | async-done | bytes 65552
  (8 shorter events, 0.1 us)
Async XLA Ops:
  7.2 44.9 %copy-start = (bf16[1,16,128,128]{3,2,1,0:T(8,128)(2,1)S(1)}, bf16[1,16,128,128]{3,2,1,0:T(8,128)(2,1)}, u32[]{:S(2)}) copy-start(bf16[1,16,128,128]{3,2,1,0:T(8,128)(2,1)} %param.11) | copy-start | bytes 1572868
  8.6 27.6 %all-to-all-start = ((s32[1,16,1]{2,0,1:T(1,128)}), s32[1,16,1]{2,0,1:T(1,128)S(1)}, u32[]{:S(2)}, u32[]{:S(2)}) async-start(s32[1,16,1]{2,0,1:T(1,128)} %copy.27), calls=%async_computation | async-start | bytes 16384 | tf_op jit(solution)/shard_map/all_to_all | solution.py:54
  42.2 5.1 copy-start.2
  42.2 545.7 %all-to-all-start.2 = ((bf16[16,384,1024]{1,2,0:T(8,128)(2,1)}), bf16[16,384,1024]{1,2,0:T(8,128)(2,1)}, u32[]{:S(2)}, u32[]{:S(2)}) async-start(bf16[16,384,1024]{1,2,0:T(8,128)(2,1)} %stack.3), calls=%async_computation.2 | async-start | bytes 25165824 | tf_op jit(solution)/shard_map/all_to_all | solution.py:36
  49.0 2.1 copy-start.4
  52.0 1.9 copy-start.1
  53.9 544.8 %copy-start.5 = (s32[1,16]{1,0:T(1,128)S(1)}, s32[1,16]{1,0:T(1,128)}, u32[]{:S(2)}) copy-start(s32[1,16]{1,0:T(1,128)} %param.12) | copy-start | bytes 196
  53.9 544.8 %copy-start.6 = (s32[1,1,16]{2,1,0:T(1,128)S(1)}, s32[1,1,16]{2,1,0:T(1,128)}, u32[]{:S(2)}) copy-start(s32[1,1,16]{2,1,0:T(1,128)} %param.15) | copy-start | bytes 196
  588.0 84.9 %all-to-all-start.1 = ((bf16[384,16,128]{2,0,1:T(8,128)(2,1)}), bf16[384,16,128]{2,0,1:T(8,128)(2,1)S(1)}, u32[]{:S(2)}, u32[]{:S(2)}) async-start(bf16[384,16,128]{2,0,1:T(8,128)(2,1)} %fusion.8), calls=%async_computation.1 | async-start | bytes 3145728 | tf_op jit(solution)/shard_map/all_to_all | solution.py:53
  598.6 116.0 %reduce-scatter.4.cloned.1.call-start = ((), (), s32[]{:S(2)}) async-start(), calls=%async_computation.4 | async-start | bytes 1114112
  614.5 6.6 copy-start.3
  625.1 50.6 %copy-start.7 = (s32[1,1,12]{2,1,0:T(1,128)S(1)}, s32[1,1,12]{2,1,0:T(1,128)}, u32[]{:S(2)}) copy-start(s32[1,1,12]{2,1,0:T(1,128)} %param.16) | copy-start | bytes 148
  673.8 8.1 %collective-permute-start.1 = (bf16[384,8,128]{2,1,0:T(8,128)(2,1)S(1)}, bf16[384,8,128]{2,1,0:T(8,128)(2,1)S(1)}, u32[]{:S(2)}, u32[]{:S(2)}) collective-permute-start(bf16[384,8,128]{2,1,0:T(8,128)(2,1)S(1)} %fusion.24), channel_id=1, source_target_pairs={{0,256},{256,0},{1,257},{257,1},{2,258},{258,2},{3,259},{259,3},{4... | collective-permute-start | bytes 2359304 | tf_op jit(solution)/shard_map/ppermute | solution.py:9
  675.8 6.2 collective-permute-start.2
  678.2 3.1 collective-permute-start
Sparse Core Ops, SparseCore 0:
  625.3 89.2 reduce-scatter.3
